TPU v7x, 32 devices: a whole 2x2x4 slice. The times are simulated.
32 devices in a mesh: row: 8 (over y, x, core), col: 4 (over z).
Axes of the slice: x: 2, y: 2, z: 4, core: 2. Of those that a mesh axis runs over, the one named last changes fastest.
Arguments:
- queries: bfloat16 [4096, 512], P(('row', 'col')), may hold values from -6 to 6
- grad_out: bfloat16 [4096, 512], P(('row', 'col')), may hold values from -6 to 6
- attn_out: bfloat16 [4096, 512], P(('row', 'col')), may hold values from -2 to 2
- key_states: bfloat16 [4096, 128], P(('row', 'col')), may hold values from -6 to 6
- value_states: bfloat16 [4096, 128], P(('row', 'col')), may hold values from -2 to 2
- log_norm: float32 [4096, 4], P(('row', 'col')), as said below
- position: int32 [4096], replicated, may hold values from 0 to 2047, as said below
- modality: int32 [4096], replicated, may hold values from 0 to 2, as said below
- bidirectional: int32 [3, 3], replicated, may hold values from 0 to 1
Outputs:
- grad_query: bfloat16 [4096, 512], P(('row', 'col'))
- grad_key: bfloat16 [4096, 128], P(('row', 'col'))
- grad_value: bfloat16 [4096, 128], P(('row', 'col'))
Inputs may be any that keep to these rules, and one draw needn't show every extreme that they name: `position`: within each sequence a permutation of 0 to 2047, token t belonging to sequence (t // 128) % 4 // 2; the tokens of one device hold two runs of 64 consecutive positions. `modality`: the same for all tokens of one sequence within one span of 32 consecutive positions. `log_norm`: the log of the number of keys that the token may see, plus 0.25 to 0.75.
All inputs are finite; a program needn't handle non-finite values.
Results may differ from a plain program's by a relative error of at most 0.0052.
Values may be sent and summed in bfloat16 or wider, within the bound.
A program may use at most 64 MiB of HBM per device.

v0:
```python
import jax
import jax.numpy as jnp
from jax import lax
from jax.sharding import PartitionSpec as P

UNIT = 64


def partner(value, axis, distance):
    mask = 2**distance
    pairs = [(source, source ^ mask) for source in range(lax.axis_size(axis))]
    return lax.ppermute(value, axis, pairs)


def shifted(block, axis, distance):
    devices = range(lax.axis_size(axis))
    route = [((i - distance) % len(devices), i) for i in devices]
    return lax.ppermute(block, axis, route)


def contract_first(left, right):
    return lax.dot_general(
        left, right, (((0,), (0,)), ((), ())), preferred_element_type=jnp.float32
    )


def contract_last(left, right):
    return lax.dot_general(
        left, right, (((1,), (1,)), ((), ())), preferred_element_type=jnp.float32
    )


def modal_hot(values):
    return (values[:, None] == jnp.arange(3, dtype=jnp.int32)[None, :]).astype(jnp.float32)


def local_tile(
    q_rows,
    d_rows,
    lse_rows,
    delta_rows,
    q_pos,
    q_mod,
    key_rows,
    value_rows,
    key_pos,
    key_mod,
    table_float,
):
    row_count = q_rows.shape[0]
    head_count = lse_rows.shape[1]
    head_width = key_rows.shape[1]
    key_count = key_rows.shape[0]
    score_scale = head_width ** (-0.5)
    flat_q = q_rows.reshape(row_count * head_count, head_width)
    flat_d = d_rows.reshape(row_count * head_count, head_width)
    scores = contract_last(flat_q, key_rows) * score_scale
    causal = key_pos[None, :] <= q_pos[:, None]
    same_unit = key_pos[None, :] // UNIT == q_pos[:, None] // UNIT
    pair_bid = contract_last(jnp.dot(modal_hot(q_mod), table_float), modal_hot(key_mod)) > 0.5
    allowed = causal | same_unit & pair_bid
    allowed = jnp.broadcast_to(allowed[:, None, :], (row_count, head_count, key_count)).reshape(
        row_count * head_count, key_count
    )
    attn_probs = jnp.where(allowed, jnp.exp(scores - lse_rows.reshape(-1, 1)), 0.0)
    probs_low = attn_probs.astype(jnp.bfloat16)
    grad_probs = contract_last(flat_d, value_rows)
    grad_scores = attn_probs * (grad_probs - delta_rows.reshape(-1, 1))
    scores_low = grad_scores.astype(jnp.bfloat16)
    grad_q = jnp.dot(scores_low, key_rows, preferred_element_type=jnp.float32) * score_scale
    grad_k = contract_first(scores_low, flat_q) * score_scale
    grad_v = contract_first(probs_low, flat_d)
    return (grad_q.reshape(row_count, head_count * head_width), grad_k, grad_v)


def shards(
    queries,
    grad_out,
    attn_out,
    key_states,
    value_states,
    log_norm,
    position,
    modality,
    bidirectional,
):
    tok_count = queries.shape[0]
    head_count = log_norm.shape[1]
    head_width = key_states.shape[1]
    row_size = lax.axis_size("row")
    col_size = lax.axis_size("col")
    row_index = lax.axis_index("row")
    col_index = lax.axis_index("col")
    parity = col_index % 2
    pair_col = col_index - parity
    row_delta = jnp.einsum(
        "thd,thd->th",
        grad_out.reshape(tok_count, head_count, head_width),
        attn_out.reshape(tok_count, head_count, head_width),
        preferred_element_type=jnp.float32,
    )
    table_float = bidirectional.astype(jnp.float32)

    def slice_meta(block_col, source, length):
        start = (source * col_size + block_col) * tok_count
        return (
            lax.dynamic_slice_in_dim(position, start, length),
            lax.dynamic_slice_in_dim(modality, start, length),
        )

    def ordered(own, other):
        first = jnp.where(parity == 0, own, other)
        second = jnp.where(parity == 0, other, own)
        return jnp.concatenate([first, second], axis=0)

    other_q, other_d = partner((queries, grad_out), "col", 0)
    other_lse, other_delta = partner((log_norm, row_delta), "col", 0)
    pair_q = ordered(queries, other_q)
    pair_d = ordered(grad_out, other_d)
    pair_lse = ordered(log_norm, other_lse)
    pair_delta = ordered(row_delta, other_delta)
    pair_pos, pair_mod = slice_meta(pair_col, row_index, 2 * tok_count)
    zero_key = jnp.zeros((tok_count, head_width), jnp.float32)
    zero_grad = jnp.zeros((2 * tok_count, head_count * head_width), jnp.float32)

    def turn_queries(step, state):
        cycle_k, cycle_v, acc_k, acc_v, acc_q = state
        source = (row_index - step) % row_size
        key_pos, key_mod = slice_meta(col_index, source, tok_count)
        grad_q, grad_k, grad_v = local_tile(
            pair_q,
            pair_d,
            pair_lse,
            pair_delta,
            pair_pos,
            pair_mod,
            cycle_k,
            cycle_v,
            key_pos,
            key_mod,
            table_float,
        )
        cycle_k, cycle_v = shifted((cycle_k, cycle_v), "row", 1)
        acc_k, acc_v = shifted((acc_k + grad_k, acc_v + grad_v), "row", 1)
        return (cycle_k, cycle_v, acc_k, acc_v, acc_q + grad_q)

    final = lax.fori_loop(
        0, row_size, turn_queries, (key_states, value_states, zero_key, zero_key, zero_grad)
    )
    got_q = partner(
        lax.dynamic_slice_in_dim(final[4], (1 - parity) * tok_count, tok_count), "col", 0
    )
    query_sum = lax.dynamic_slice_in_dim(final[4], parity * tok_count, tok_count) + got_q
    key_sum = final[2]
    value_sum = final[3]
    return (
        query_sum.astype(jnp.bfloat16),
        key_sum.astype(jnp.bfloat16),
        value_sum.astype(jnp.bfloat16),
    )


def solution(mesh):
    return jax.shard_map(
        shards,
        mesh=mesh,
        in_specs=(
            P(("row", "col"), None),
            P(("row", "col"), None),
            P(("row", "col"), None),
            P(("row", "col"), None),
            P(("row", "col"), None),
            P(("row", "col"), None),
            P(),
            P(),
            P(),
        ),
        out_specs=(P(("row", "col"), None), P(("row", "col"), None), P(("row", "col"), None)),
        check_vma=False,
    )
```

profile of v0, /device:TPU:0, one launch (start us, length us, event | category | flops | bytes accessed | tf_op | source)
XLA Modules:
  0.0 96.6 jit_solution(16556188526686403017)
XLA Ops:
  0.6 3.1 %collective-permute-start.4 = (bf16[128,512]{1,0:T(8,128)(2,1)}, bf16[128,512]{1,0:T(8,128)(2,1)S(1)}, u32[]{:S(2)}, u32[]{:S(2)}) collective-permute-start(bf16[128,512]{1,0:T(8,128)(2,1)} %param.11), channel_id=1, source_target_pairs={{0,1},{1,0},{2,3},{3,2},{4,5},{5,4},{6,7},{7,6},{8,9},{9,8},{10,11... | collective-permute-start | bytes 393224 | tf_op jit(solution)/shard_map/ppermute | solution.py:12
  3.8 1.0 %reshape.144 = bf16[128,4,128]{2,1,0:T(4,128)(2,1)S(1)} reshape(bf16[128,512]{1,0:T(8,128)(2,1)} %param.12) | data formatting | bytes 262144 | tf_op jit(solution)/shard_map/reshape | solution.py:98
  5.1 2.0 %collective-permute-start.7 = (f32[128,4]{0,1:T(4,128)S(1)}, f32[128,4]{0,1:T(4,128)S(1)}, u32[]{:S(2)}, u32[]{:S(2)}) collective-permute-start(f32[128,4]{0,1:T(4,128)S(1)} %copy.21), channel_id=1, source_target_pairs={{0,1},{1,0},{2,3},{3,2},{4,5},{5,4},{6,7},{7,6},{8,9},{9,8},{10,11... | collective-permute-start | bytes 6152 | tf_op jit(solution)/shard_map/ppermute | solution.py:12
  7.1 0.6 collective-permute-start.5
  7.7 0.8 fusion.15
  8.5 0.8 dynamic_slice.35
  9.2 1.1 %collective-permute-done.7 = f32[128,4]{0,1:T(4,128)S(1)} collective-permute-done((f32[128,4]{0,1:T(4,128)S(1)}, f32[128,4]{0,1:T(4,128)S(1)}, u32[]{:S(2)}, u32[]{:S(2)}) %collective-permute-start.7) | collective-permute-done | bytes 2080 | tf_op jit(solution)/shard_map/ppermute | solution.py:12
  12.0 0.6 copy-done.4
  12.8 0.5 copy-done.2
  13.7 0.7 copy-done
  14.4 74.4 %while.26 = (s32[]{:T(128)}, bf16[128,128]{1,0:T(8,128)(2,1)S(1)}, bf16[128,128]{1,0:T(8,128)(2,1)S(1)}, f32[128,128]{1,0:T(8,128)S(1)}, f32[128,128]{1,0:T(8,12...) while((s32[]{:T(128)}, bf16[128,128]{1,0:T(8,128)(2,1)S(1)}, ...), condition=%wide.wide.region_1.2_spmd.clone, body=%wide.wide.region_0.1_spmd.clone.sunk | while | flops 169503504 | bytes 8179848 | solution.py:147
  14.4 1.6 %collective-permute-start.1 = (bf16[128,128]{1,0:T(8,128)(2,1)S(1)}, bf16[128,128]{1,0:T(8,128)(2,1)S(1)}, u32[]{:S(2)}, u32[]{:S(2)}) collective-permute-start(bf16[128,128]{1,0:T(8,128)(2,1)S(1)} %copy.31), channel_id=1, source_target_pairs={{28,0},{0,4},{4,8},{8,12},{12,16},{16,20},{20,24},{24,28},{29,1},{... | collective-permute-start | bytes 98312 | tf_op jit(solution)/shard_map/while/body/eval_jaxpr/ppermute | solution.py:18
  16.1 0.8 and_select_fusion.6
  16.8 0.8 dynamic_slice.49
  19.4 1.6 %collective-permute-start.3 = (f32[128,128]{1,0:T(8,128)S(1)}, f32[128,128]{1,0:T(8,128)S(1)}, u32[]{:S(2)}, u32[]{:S(2)}) collective-permute-start(f32[128,128]{1,0:T(8,128)S(1)} %convolution_add_fusion.3), channel_id=1, source_target_pairs={{28,0},{0,4},{4,8},{8,12},{12,16},{16,20},{20,24},{24,28},{29,1},{... | collective-permute-start | bytes 196616 | tf_op jit(solution)/shard_map/while/body/eval_jaxpr/ppermute | solution.py:18
  21.5 2.1 %collective-permute-done.2 = f32[128,128]{1,0:T(8,128)S(1)} collective-permute-done((f32[128,128]{1,0:T(8,128)S(1)}, f32[128,128]{1,0:T(8,128)S(1)}, u32[]{:S(2)}, u32[]{:S(2)}) %collective-permute-start.2) | collective-permute-done | bytes 65568 | tf_op jit(solution)/shard_map/while/body/eval_jaxpr/ppermute | solution.py:18
  23.7 0.7 collective-permute-done.3
  24.4 0.7 collective-permute-start.1
  25.1 0.8 and_select_fusion.6
  25.9 0.8 dynamic_slice.49
  26.7 0.5 fusion.70
  28.5 2.5 %collective-permute-start.3 = (f32[128,128]{1,0:T(8,128)S(1)}, f32[128,128]{1,0:T(8,128)S(1)}, u32[]{:S(2)}, u32[]{:S(2)}) collective-permute-start(f32[128,128]{1,0:T(8,128)S(1)} %convolution_add_fusion.3), channel_id=1, source_target_pairs={{28,0},{0,4},{4,8},{8,12},{12,16},{16,20},{20,24},{24,28},{29,1},{... | collective-permute-start | bytes 196616 | tf_op jit(solution)/shard_map/while/body/eval_jaxpr/ppermute | solution.py:18
  31.5 1.2 %collective-permute-done.2 = f32[128,128]{1,0:T(8,128)S(1)} collective-permute-done((f32[128,128]{1,0:T(8,128)S(1)}, f32[128,128]{1,0:T(8,128)S(1)}, u32[]{:S(2)}, u32[]{:S(2)}) %collective-permute-start.2) | collective-permute-done | bytes 65568 | tf_op jit(solution)/shard_map/while/body/eval_jaxpr/ppermute | solution.py:18
  32.7 0.7 collective-permute-done.3
  33.4 1.6 %collective-permute-start.1 = (bf16[128,128]{1,0:T(8,128)(2,1)S(1)}, bf16[128,128]{1,0:T(8,128)(2,1)S(1)}, u32[]{:S(2)}, u32[]{:S(2)}) collective-permute-start(bf16[128,128]{1,0:T(8,128)(2,1)S(1)} %copy.31), channel_id=1, source_target_pairs={{28,0},{0,4},{4,8},{8,12},{12,16},{16,20},{20,24},{24,28},{29,1},{... | collective-permute-start | bytes 98312 | tf_op jit(solution)/shard_map/while/body/eval_jaxpr/ppermute | solution.py:18
  35.1 0.8 and_select_fusion.6
  35.8 0.8 dynamic_slice.49
  36.6 0.5 fusion.70
  38.4 1.0 %collective-permute-start.3 = (f32[128,128]{1,0:T(8,128)S(1)}, f32[128,128]{1,0:T(8,128)S(1)}, u32[]{:S(2)}, u32[]{:S(2)}) collective-permute-start(f32[128,128]{1,0:T(8,128)S(1)} %convolution_add_fusion.3), channel_id=1, source_target_pairs={{28,0},{0,4},{4,8},{8,12},{12,16},{16,20},{20,24},{24,28},{29,1},{... | collective-permute-start | bytes 196616 | tf_op jit(solution)/shard_map/while/body/eval_jaxpr/ppermute | solution.py:18
  39.9 2.7 %collective-permute-done.2 = f32[128,128]{1,0:T(8,128)S(1)} collective-permute-done((f32[128,128]{1,0:T(8,128)S(1)}, f32[128,128]{1,0:T(8,128)S(1)}, u32[]{:S(2)}, u32[]{:S(2)}) %collective-permute-start.2) | collective-permute-done | bytes 65568 | tf_op jit(solution)/shard_map/while/body/eval_jaxpr/ppermute | solution.py:18
  42.7 0.7 collective-permute-done.3
  43.5 0.8 and_select_fusion.6
  44.3 0.8 dynamic_slice.49
  46.9 2.1 %collective-permute-start.3 = (f32[128,128]{1,0:T(8,128)S(1)}, f32[128,128]{1,0:T(8,128)S(1)}, u32[]{:S(2)}, u32[]{:S(2)}) collective-permute-start(f32[128,128]{1,0:T(8,128)S(1)} %convolution_add_fusion.3), channel_id=1, source_target_pairs={{28,0},{0,4},{4,8},{8,12},{12,16},{16,20},{20,24},{24,28},{29,1},{... | collective-permute-start | bytes 196616 | tf_op jit(solution)/shard_map/while/body/eval_jaxpr/ppermute | solution.py:18
  49.5 1.6 %collective-permute-done.2 = f32[128,128]{1,0:T(8,128)S(1)} collective-permute-done((f32[128,128]{1,0:T(8,128)S(1)}, f32[128,128]{1,0:T(8,128)S(1)}, u32[]{:S(2)}, u32[]{:S(2)}) %collective-permute-start.2) | collective-permute-done | bytes 65568 | tf_op jit(solution)/shard_map/while/body/eval_jaxpr/ppermute | solution.py:18
  51.1 0.7 collective-permute-done.3
  51.8 1.2 %collective-permute-start.1 = (bf16[128,128]{1,0:T(8,128)(2,1)S(1)}, bf16[128,128]{1,0:T(8,128)(2,1)S(1)}, u32[]{:S(2)}, u32[]{:S(2)}) collective-permute-start(bf16[128,128]{1,0:T(8,128)(2,1)S(1)} %copy.31), channel_id=1, source_target_pairs={{28,0},{0,4},{4,8},{8,12},{12,16},{16,20},{20,24},{24,28},{29,1},{... | collective-permute-start | bytes 98312 | tf_op jit(solution)/shard_map/while/body/eval_jaxpr/ppermute | solution.py:18
  53.1 0.8 and_select_fusion.6
  53.8 0.8 dynamic_slice.49
  56.4 1.6 %collective-permute-start.3 = (f32[128,128]{1,0:T(8,128)S(1)}, f32[128,128]{1,0:T(8,128)S(1)}, u32[]{:S(2)}, u32[]{:S(2)}) collective-permute-start(f32[128,128]{1,0:T(8,128)S(1)} %convolution_add_fusion.3), channel_id=1, source_target_pairs={{28,0},{0,4},{4,8},{8,12},{12,16},{16,20},{20,24},{24,28},{29,1},{... | collective-permute-start | bytes 196616 | tf_op jit(solution)/shard_map/while/body/eval_jaxpr/ppermute | solution.py:18
  58.5 2.1 %collective-permute-done.2 = f32[128,128]{1,0:T(8,128)S(1)} collective-permute-done((f32[128,128]{1,0:T(8,128)S(1)}, f32[128,128]{1,0:T(8,128)S(1)}, u32[]{:S(2)}, u32[]{:S(2)}) %collective-permute-start.2) | collective-permute-done | bytes 65568 | tf_op jit(solution)/shard_map/while/body/eval_jaxpr/ppermute | solution.py:18
  60.7 0.7 collective-permute-done.3
  61.4 0.7 collective-permute-start.1
  62.1 0.8 and_select_fusion.6
  62.9 0.8 dynamic_slice.49
  65.5 2.5 %collective-permute-start.3 = (f32[128,128]{1,0:T(8,128)S(1)}, f32[128,128]{1,0:T(8,128)S(1)}, u32[]{:S(2)}, u32[]{:S(2)}) collective-permute-start(f32[128,128]{1,0:T(8,128)S(1)} %convolution_add_fusion.3), channel_id=1, source_target_pairs={{28,0},{0,4},{4,8},{8,12},{12,16},{16,20},{20,24},{24,28},{29,1},{... | collective-permute-start | bytes 196616 | tf_op jit(solution)/shard_map/while/body/eval_jaxpr/ppermute | solution.py:18
  68.5 1.2 %collective-permute-done.2 = f32[128,128]{1,0:T(8,128)S(1)} collective-permute-done((f32[128,128]{1,0:T(8,128)S(1)}, f32[128,128]{1,0:T(8,128)S(1)}, u32[]{:S(2)}, u32[]{:S(2)}) %collective-permute-start.2) | collective-permute-done | bytes 65568 | tf_op jit(solution)/shard_map/while/body/eval_jaxpr/ppermute | solution.py:18
  69.7 0.7 collective-permute-done.3
  70.4 1.6 %collective-permute-start.1 = (bf16[128,128]{1,0:T(8,128)(2,1)S(1)}, bf16[128,128]{1,0:T(8,128)(2,1)S(1)}, u32[]{:S(2)}, u32[]{:S(2)}) collective-permute-start(bf16[128,128]{1,0:T(8,128)(2,1)S(1)} %copy.31), channel_id=1, source_target_pairs={{28,0},{0,4},{4,8},{8,12},{12,16},{16,20},{20,24},{24,28},{29,1},{... | collective-permute-start | bytes 98312 | tf_op jit(solution)/shard_map/while/body/eval_jaxpr/ppermute | solution.py:18
  72.1 0.8 and_select_fusion.6
  72.8 0.8 dynamic_slice.49
  75.4 1.0 %collective-permute-start.3 = (f32[128,128]{1,0:T(8,128)S(1)}, f32[128,128]{1,0:T(8,128)S(1)}, u32[]{:S(2)}, u32[]{:S(2)}) collective-permute-start(f32[128,128]{1,0:T(8,128)S(1)} %convolution_add_fusion.3), channel_id=1, source_target_pairs={{28,0},{0,4},{4,8},{8,12},{12,16},{16,20},{20,24},{24,28},{29,1},{... | collective-permute-start | bytes 196616 | tf_op jit(solution)/shard_map/while/body/eval_jaxpr/ppermute | solution.py:18
  76.9 2.7 %collective-permute-done.2 = f32[128,128]{1,0:T(8,128)S(1)} collective-permute-done((f32[128,128]{1,0:T(8,128)S(1)}, f32[128,128]{1,0:T(8,128)S(1)}, u32[]{:S(2)}, u32[]{:S(2)}) %collective-permute-start.2) | collective-permute-done | bytes 65568 | tf_op jit(solution)/shard_map/while/body/eval_jaxpr/ppermute | solution.py:18
  79.7 0.7 collective-permute-done.3
  80.5 0.8 and_select_fusion.6
  81.3 0.8 dynamic_slice.49
  83.9 2.1 %collective-permute-start.3 = (f32[128,128]{1,0:T(8,128)S(1)}, f32[128,128]{1,0:T(8,128)S(1)}, u32[]{:S(2)}, u32[]{:S(2)}) collective-permute-start(f32[128,128]{1,0:T(8,128)S(1)} %convolution_add_fusion.3), channel_id=1, source_target_pairs={{28,0},{0,4},{4,8},{8,12},{12,16},{16,20},{20,24},{24,28},{29,1},{... | collective-permute-start | bytes 196616 | tf_op jit(solution)/shard_map/while/body/eval_jaxpr/ppermute | solution.py:18
  86.5 1.6 %collective-permute-done.2 = f32[128,128]{1,0:T(8,128)S(1)} collective-permute-done((f32[128,128]{1,0:T(8,128)S(1)}, f32[128,128]{1,0:T(8,128)S(1)}, u32[]{:S(2)}, u32[]{:S(2)}) %collective-permute-start.2) | collective-permute-done | bytes 65568 | tf_op jit(solution)/shard_map/while/body/eval_jaxpr/ppermute | solution.py:18
  88.1 0.7 collective-permute-done.3
  88.8 1.5 %collective-permute-start.8 = (f32[128,512]{1,0:T(8,128)S(1)}, f32[128,512]{1,0:T(8,128)S(1)}, u32[]{:S(2)}, u32[]{:S(2)}) collective-permute-start(f32[128,512]{1,0:T(8,128)S(1)} %constant_dynamic-slice_fusion), channel_id=1, source_target_pairs={{0,1},{1,0},{2,3},{3,2},{4,5},{5,4},{6,7},{7,6},{8,9},{9,8},{10,11... | collective-permute-start | bytes 786440 | tf_op jit(solution)/shard_map/ppermute | solution.py:12
  90.3 0.6 convert_element_type.42
  90.9 0.6 convert_element_type.43
  91.5 4.3 %collective-permute-done.8 = f32[128,512]{1,0:T(8,128)S(1)} collective-permute-done((f32[128,512]{1,0:T(8,128)S(1)}, f32[128,512]{1,0:T(8,128)S(1)}, u32[]{:S(2)}, u32[]{:S(2)}) %collective-permute-start.8) | collective-permute-done | bytes 262176 | tf_op jit(solution)/shard_map/ppermute | solution.py:12
  95.9 0.7 add_convert_fusion
  (180 shorter events, 20.2 us)
Async XLA Ops:
  0.6 4.2 %copy-start.8 = (bf16[128,512]{1,0:T(8,128)(2,1)S(1)}, bf16[128,512]{1,0:T(8,128)(2,1)}, u32[]{:S(2)}) copy-start(bf16[128,512]{1,0:T(8,128)(2,1)} %param.13) | copy-start | bytes 393220
  0.6 11.0 %collective-permute-start.4 = (bf16[128,512]{1,0:T(8,128)(2,1)}, bf16[128,512]{1,0:T(8,128)(2,1)S(1)}, u32[]{:S(2)}, u32[]{:S(2)}) collective-permute-start(bf16[128,512]{1,0:T(8,128)(2,1)} %param.11), channel_id=1, source_target_pairs={{0,1},{1,0},{2,3},{3,2},{4,5},{5,4},{6,7},{7,6},{8,9},{9,8},{10,11... | collective-permute-start | bytes 393224 | tf_op jit(solution)/shard_map/ppermute | solution.py:12
  3.7 8.3 %collective-permute-start.6 = (bf16[128,512]{1,0:T(8,128)(2,1)}, bf16[128,512]{1,0:T(8,128)(2,1)S(1)}, u32[]{:S(2)}, u32[]{:S(2)}) collective-permute-start(bf16[128,512]{1,0:T(8,128)(2,1)} %param.12), channel_id=1, source_target_pairs={{0,1},{1,0},{2,3},{3,2},{4,5},{5,4},{6,7},{7,6},{8,9},{9,8},{10,11... | collective-permute-start | bytes 393224 | tf_op jit(solution)/shard_map/ppermute | solution.py:12
  5.0 2.0 %copy-start.9 = (f32[128,4]{0,1:T(4,128)S(1)}, f32[128,4]{0,1:T(4,128)}, u32[]{:S(2)}) copy-start(f32[128,4]{0,1:T(4,128)} %param.16) | copy-start | bytes 6148
  5.1 5.2 %collective-permute-start.7 = (f32[128,4]{0,1:T(4,128)S(1)}, f32[128,4]{0,1:T(4,128)S(1)}, u32[]{:S(2)}, u32[]{:S(2)}) collective-permute-start(f32[128,4]{0,1:T(4,128)S(1)} %copy.21), channel_id=1, source_target_pairs={{0,1},{1,0},{2,3},{3,2},{4,5},{5,4},{6,7},{7,6},{8,9},{9,8},{10,11... | collective-permute-start | bytes 6152 | tf_op jit(solution)/shard_map/ppermute | solution.py:12
  7.1 3.6 %collective-permute-start.5 = (f32[128,4]{0,1:T(4,128)S(1)}, f32[128,4]{0,1:T(4,128)S(1)}, u32[]{:S(2)}, u32[]{:S(2)}) collective-permute-start(f32[128,4]{0,1:T(4,128)S(1)} %copy-done.9), channel_id=1, source_target_pairs={{0,1},{1,0},{2,3},{3,2},{4,5},{5,4},{6,7},{7,6},{8,9},{9,8},{10,11... | collective-permute-start | bytes 6152 | tf_op jit(solution)/shard_map/ppermute | solution.py:12
  8.5 0.8 copy-start.10
  10.8 0.7 copy-start.5
  11.0 0.7 copy-start.6
  11.0 1.0 copy-start.7
  11.7 0.9 copy-start.4
  12.7 0.7 copy-start.2
  12.7 0.8 copy-start.3
  13.6 0.8 copy-start
  13.7 0.8 copy-start.1
  14.4 7.1 %collective-permute-start = (bf16[128,128]{1,0:T(8,128)(2,1)S(1)}, bf16[128,128]{1,0:T(8,128)(2,1)S(1)}, u32[]{:S(2)}, u32[]{:S(2)}) collective-permute-start(bf16[128,128]{1,0:T(8,128)(2,1)S(1)} %copy.30), channel_id=1, source_target_pairs={{28,0},{0,4},{4,8},{8,12},{12,16},{16,20},{20,24},{24,28},{29,1},{... | collective-permute-start | bytes 98312 | tf_op jit(solution)/shard_map/while/body/eval_jaxpr/ppermute | solution.py:18
  14.4 7.1 %collective-permute-start.1 = (bf16[128,128]{1,0:T(8,128)(2,1)S(1)}, bf16[128,128]{1,0:T(8,128)(2,1)S(1)}, u32[]{:S(2)}, u32[]{:S(2)}) collective-permute-start(bf16[128,128]{1,0:T(8,128)(2,1)S(1)} %copy.31), channel_id=1, source_target_pairs={{28,0},{0,4},{4,8},{8,12},{12,16},{16,20},{20,24},{24,28},{29,1},{... | collective-permute-start | bytes 98312 | tf_op jit(solution)/shard_map/while/body/eval_jaxpr/ppermute | solution.py:18
  19.0 4.6 %collective-permute-start.2 = (f32[128,128]{1,0:T(8,128)S(1)}, f32[128,128]{1,0:T(8,128)S(1)}, u32[]{:S(2)}, u32[]{:S(2)}) collective-permute-start(f32[128,128]{1,0:T(8,128)S(1)} %fusion.73), channel_id=1, source_target_pairs={{28,0},{0,4},{4,8},{8,12},{12,16},{16,20},{20,24},{24,28},{29,1},{... | collective-permute-start | bytes 196616 | tf_op jit(solution)/shard_map/while/body/eval_jaxpr/ppermute | solution.py:18
  19.4 5.0 %collective-permute-start.3 = (f32[128,128]{1,0:T(8,128)S(1)}, f32[128,128]{1,0:T(8,128)S(1)}, u32[]{:S(2)}, u32[]{:S(2)}) collective-permute-start(f32[128,128]{1,0:T(8,128)S(1)} %convolution_add_fusion.3), channel_id=1, source_target_pairs={{28,0},{0,4},{4,8},{8,12},{12,16},{16,20},{20,24},{24,28},{29,1},{... | collective-permute-start | bytes 196616 | tf_op jit(solution)/shard_map/while/body/eval_jaxpr/ppermute | solution.py:18
  24.4 7.1 %collective-permute-start = (bf16[128,128]{1,0:T(8,128)(2,1)S(1)}, bf16[128,128]{1,0:T(8,128)(2,1)S(1)}, u32[]{:S(2)}, u32[]{:S(2)}) collective-permute-start(bf16[128,128]{1,0:T(8,128)(2,1)S(1)} %copy.30), channel_id=1, source_target_pairs={{28,0},{0,4},{4,8},{8,12},{12,16},{16,20},{20,24},{24,28},{29,1},{... | collective-permute-start | bytes 98312 | tf_op jit(solution)/shard_map/while/body/eval_jaxpr/ppermute | solution.py:18
  24.4 7.1 %collective-permute-start.1 = (bf16[128,128]{1,0:T(8,128)(2,1)S(1)}, bf16[128,128]{1,0:T(8,128)(2,1)S(1)}, u32[]{:S(2)}, u32[]{:S(2)}) collective-permute-start(bf16[128,128]{1,0:T(8,128)(2,1)S(1)} %copy.31), channel_id=1, source_target_pairs={{28,0},{0,4},{4,8},{8,12},{12,16},{16,20},{20,24},{24,28},{29,1},{... | collective-permute-start | bytes 98312 | tf_op jit(solution)/shard_map/while/body/eval_jaxpr/ppermute | solution.py:18
  28.1 4.6 %collective-permute-start.2 = (f32[128,128]{1,0:T(8,128)S(1)}, f32[128,128]{1,0:T(8,128)S(1)}, u32[]{:S(2)}, u32[]{:S(2)}) collective-permute-start(f32[128,128]{1,0:T(8,128)S(1)} %fusion.73), channel_id=1, source_target_pairs={{28,0},{0,4},{4,8},{8,12},{12,16},{16,20},{20,24},{24,28},{29,1},{... | collective-permute-start | bytes 196616 | tf_op jit(solution)/shard_map/while/body/eval_jaxpr/ppermute | solution.py:18
  28.5 5.0 %collective-permute-start.3 = (f32[128,128]{1,0:T(8,128)S(1)}, f32[128,128]{1,0:T(8,128)S(1)}, u32[]{:S(2)}, u32[]{:S(2)}) collective-permute-start(f32[128,128]{1,0:T(8,128)S(1)} %convolution_add_fusion.3), channel_id=1, source_target_pairs={{28,0},{0,4},{4,8},{8,12},{12,16},{16,20},{20,24},{24,28},{29,1},{... | collective-permute-start | bytes 196616 | tf_op jit(solution)/shard_map/while/body/eval_jaxpr/ppermute | solution.py:18
  33.4 6.5 %collective-permute-start = (bf16[128,128]{1,0:T(8,128)(2,1)S(1)}, bf16[128,128]{1,0:T(8,128)(2,1)S(1)}, u32[]{:S(2)}, u32[]{:S(2)}) collective-permute-start(bf16[128,128]{1,0:T(8,128)(2,1)S(1)} %copy.30), channel_id=1, source_target_pairs={{28,0},{0,4},{4,8},{8,12},{12,16},{16,20},{20,24},{24,28},{29,1},{... | collective-permute-start | bytes 98312 | tf_op jit(solution)/shard_map/while/body/eval_jaxpr/ppermute | solution.py:18
  33.4 6.5 %collective-permute-start.1 = (bf16[128,128]{1,0:T(8,128)(2,1)S(1)}, bf16[128,128]{1,0:T(8,128)(2,1)S(1)}, u32[]{:S(2)}, u32[]{:S(2)}) collective-permute-start(bf16[128,128]{1,0:T(8,128)(2,1)S(1)} %copy.31), channel_id=1, source_target_pairs={{28,0},{0,4},{4,8},{8,12},{12,16},{16,20},{20,24},{24,28},{29,1},{... | collective-permute-start | bytes 98312 | tf_op jit(solution)/shard_map/while/body/eval_jaxpr/ppermute | solution.py:18
  38.0 4.6 %collective-permute-start.2 = (f32[128,128]{1,0:T(8,128)S(1)}, f32[128,128]{1,0:T(8,128)S(1)}, u32[]{:S(2)}, u32[]{:S(2)}) collective-permute-start(f32[128,128]{1,0:T(8,128)S(1)} %fusion.73), channel_id=1, source_target_pairs={{28,0},{0,4},{4,8},{8,12},{12,16},{16,20},{20,24},{24,28},{29,1},{... | collective-permute-start | bytes 196616 | tf_op jit(solution)/shard_map/while/body/eval_jaxpr/ppermute | solution.py:18
  38.4 5.0 %collective-permute-start.3 = (f32[128,128]{1,0:T(8,128)S(1)}, f32[128,128]{1,0:T(8,128)S(1)}, u32[]{:S(2)}, u32[]{:S(2)}) collective-permute-start(f32[128,128]{1,0:T(8,128)S(1)} %convolution_add_fusion.3), channel_id=1, source_target_pairs={{28,0},{0,4},{4,8},{8,12},{12,16},{16,20},{20,24},{24,28},{29,1},{... | collective-permute-start | bytes 196616 | tf_op jit(solution)/shard_map/while/body/eval_jaxpr/ppermute | solution.py:18
  43.4 6.1 %collective-permute-start = (bf16[128,128]{1,0:T(8,128)(2,1)S(1)}, bf16[128,128]{1,0:T(8,128)(2,1)S(1)}, u32[]{:S(2)}, u32[]{:S(2)}) collective-permute-start(bf16[128,128]{1,0:T(8,128)(2,1)S(1)} %copy.30), channel_id=1, source_target_pairs={{28,0},{0,4},{4,8},{8,12},{12,16},{16,20},{20,24},{24,28},{29,1},{... | collective-permute-start | bytes 98312 | tf_op jit(solution)/shard_map/while/body/eval_jaxpr/ppermute | solution.py:18
  43.4 6.1 %collective-permute-start.1 = (bf16[128,128]{1,0:T(8,128)(2,1)S(1)}, bf16[128,128]{1,0:T(8,128)(2,1)S(1)}, u32[]{:S(2)}, u32[]{:S(2)}) collective-permute-start(bf16[128,128]{1,0:T(8,128)(2,1)S(1)} %copy.31), channel_id=1, source_target_pairs={{28,0},{0,4},{4,8},{8,12},{12,16},{16,20},{20,24},{24,28},{29,1},{... | collective-permute-start | bytes 98312 | tf_op jit(solution)/shard_map/while/body/eval_jaxpr/ppermute | solution.py:18
  46.5 4.6 %collective-permute-start.2 = (f32[128,128]{1,0:T(8,128)S(1)}, f32[128,128]{1,0:T(8,128)S(1)}, u32[]{:S(2)}, u32[]{:S(2)}) collective-permute-start(f32[128,128]{1,0:T(8,128)S(1)} %fusion.73), channel_id=1, source_target_pairs={{28,0},{0,4},{4,8},{8,12},{12,16},{16,20},{20,24},{24,28},{29,1},{... | collective-permute-start | bytes 196616 | tf_op jit(solution)/shard_map/while/body/eval_jaxpr/ppermute | solution.py:18
  46.9 5.0 %collective-permute-start.3 = (f32[128,128]{1,0:T(8,128)S(1)}, f32[128,128]{1,0:T(8,128)S(1)}, u32[]{:S(2)}, u32[]{:S(2)}) collective-permute-start(f32[128,128]{1,0:T(8,128)S(1)} %convolution_add_fusion.3), channel_id=1, source_target_pairs={{28,0},{0,4},{4,8},{8,12},{12,16},{16,20},{20,24},{24,28},{29,1},{... | collective-permute-start | bytes 196616 | tf_op jit(solution)/shard_map/while/body/eval_jaxpr/ppermute | solution.py:18
  51.8 6.7 %collective-permute-start = (bf16[128,128]{1,0:T(8,128)(2,1)S(1)}, bf16[128,128]{1,0:T(8,128)(2,1)S(1)}, u32[]{:S(2)}, u32[]{:S(2)}) collective-permute-start(bf16[128,128]{1,0:T(8,128)(2,1)S(1)} %copy.30), channel_id=1, source_target_pairs={{28,0},{0,4},{4,8},{8,12},{12,16},{16,20},{20,24},{24,28},{29,1},{... | collective-permute-start | bytes 98312 | tf_op jit(solution)/shard_map/while/body/eval_jaxpr/ppermute | solution.py:18
  51.8 6.7 %collective-permute-start.1 = (bf16[128,128]{1,0:T(8,128)(2,1)S(1)}, bf16[128,128]{1,0:T(8,128)(2,1)S(1)}, u32[]{:S(2)}, u32[]{:S(2)}) collective-permute-start(bf16[128,128]{1,0:T(8,128)(2,1)S(1)} %copy.31), channel_id=1, source_target_pairs={{28,0},{0,4},{4,8},{8,12},{12,16},{16,20},{20,24},{24,28},{29,1},{... | collective-permute-start | bytes 98312 | tf_op jit(solution)/shard_map/while/body/eval_jaxpr/ppermute | solution.py:18
  56.0 4.6 %collective-permute-start.2 = (f32[128,128]{1,0:T(8,128)S(1)}, f32[128,128]{1,0:T(8,128)S(1)}, u32[]{:S(2)}, u32[]{:S(2)}) collective-permute-start(f32[128,128]{1,0:T(8,128)S(1)} %fusion.73), channel_id=1, source_target_pairs={{28,0},{0,4},{4,8},{8,12},{12,16},{16,20},{20,24},{24,28},{29,1},{... | collective-permute-start | bytes 196616 | tf_op jit(solution)/shard_map/while/body/eval_jaxpr/ppermute | solution.py:18
  56.4 5.0 %collective-permute-start.3 = (f32[128,128]{1,0:T(8,128)S(1)}, f32[128,128]{1,0:T(8,128)S(1)}, u32[]{:S(2)}, u32[]{:S(2)}) collective-permute-start(f32[128,128]{1,0:T(8,128)S(1)} %convolution_add_fusion.3), channel_id=1, source_target_pairs={{28,0},{0,4},{4,8},{8,12},{12,16},{16,20},{20,24},{24,28},{29,1},{... | collective-permute-start | bytes 196616 | tf_op jit(solution)/shard_map/while/body/eval_jaxpr/ppermute | solution.py:18
  61.4 7.1 %collective-permute-start = (bf16[128,128]{1,0:T(8,128)(2,1)S(1)}, bf16[128,128]{1,0:T(8,128)(2,1)S(1)}, u32[]{:S(2)}, u32[]{:S(2)}) collective-permute-start(bf16[128,128]{1,0:T(8,128)(2,1)S(1)} %copy.30), channel_id=1, source_target_pairs={{28,0},{0,4},{4,8},{8,12},{12,16},{16,20},{20,24},{24,28},{29,1},{... | collective-permute-start | bytes 98312 | tf_op jit(solution)/shard_map/while/body/eval_jaxpr/ppermute | solution.py:18
  61.4 7.1 %collective-permute-start.1 = (bf16[128,128]{1,0:T(8,128)(2,1)S(1)}, bf16[128,128]{1,0:T(8,128)(2,1)S(1)}, u32[]{:S(2)}, u32[]{:S(2)}) collective-permute-start(bf16[128,128]{1,0:T(8,128)(2,1)S(1)} %copy.31), channel_id=1, source_target_pairs={{28,0},{0,4},{4,8},{8,12},{12,16},{16,20},{20,24},{24,28},{29,1},{... | collective-permute-start | bytes 98312 | tf_op jit(solution)/shard_map/while/body/eval_jaxpr/ppermute | solution.py:18
  65.1 4.6 %collective-permute-start.2 = (f32[128,128]{1,0:T(8,128)S(1)}, f32[128,128]{1,0:T(8,128)S(1)}, u32[]{:S(2)}, u32[]{:S(2)}) collective-permute-start(f32[128,128]{1,0:T(8,128)S(1)} %fusion.73), channel_id=1, source_target_pairs={{28,0},{0,4},{4,8},{8,12},{12,16},{16,20},{20,24},{24,28},{29,1},{... | collective-permute-start | bytes 196616 | tf_op jit(solution)/shard_map/while/body/eval_jaxpr/ppermute | solution.py:18
  65.5 5.0 %collective-permute-start.3 = (f32[128,128]{1,0:T(8,128)S(1)}, f32[128,128]{1,0:T(8,128)S(1)}, u32[]{:S(2)}, u32[]{:S(2)}) collective-permute-start(f32[128,128]{1,0:T(8,128)S(1)} %convolution_add_fusion.3), channel_id=1, source_target_pairs={{28,0},{0,4},{4,8},{8,12},{12,16},{16,20},{20,24},{24,28},{29,1},{... | collective-permute-start | bytes 196616 | tf_op jit(solution)/shard_map/while/body/eval_jaxpr/ppermute | solution.py:18
  70.4 6.5 %collective-permute-start = (bf16[128,128]{1,0:T(8,128)(2,1)S(1)}, bf16[128,128]{1,0:T(8,128)(2,1)S(1)}, u32[]{:S(2)}, u32[]{:S(2)}) collective-permute-start(bf16[128,128]{1,0:T(8,128)(2,1)S(1)} %copy.30), channel_id=1, source_target_pairs={{28,0},{0,4},{4,8},{8,12},{12,16},{16,20},{20,24},{24,28},{29,1},{... | collective-permute-start | bytes 98312 | tf_op jit(solution)/shard_map/while/body/eval_jaxpr/ppermute | solution.py:18
  70.4 6.5 %collective-permute-start.1 = (bf16[128,128]{1,0:T(8,128)(2,1)S(1)}, bf16[128,128]{1,0:T(8,128)(2,1)S(1)}, u32[]{:S(2)}, u32[]{:S(2)}) collective-permute-start(bf16[128,128]{1,0:T(8,128)(2,1)S(1)} %copy.31), channel_id=1, source_target_pairs={{28,0},{0,4},{4,8},{8,12},{12,16},{16,20},{20,24},{24,28},{29,1},{... | collective-permute-start | bytes 98312 | tf_op jit(solution)/shard_map/while/body/eval_jaxpr/ppermute | solution.py:18
  75.0 4.6 %collective-permute-start.2 = (f32[128,128]{1,0:T(8,128)S(1)}, f32[128,128]{1,0:T(8,128)S(1)}, u32[]{:S(2)}, u32[]{:S(2)}) collective-permute-start(f32[128,128]{1,0:T(8,128)S(1)} %fusion.73), channel_id=1, source_target_pairs={{28,0},{0,4},{4,8},{8,12},{12,16},{16,20},{20,24},{24,28},{29,1},{... | collective-permute-start | bytes 196616 | tf_op jit(solution)/shard_map/while/body/eval_jaxpr/ppermute | solution.py:18
  75.4 5.0 %collective-permute-start.3 = (f32[128,128]{1,0:T(8,128)S(1)}, f32[128,128]{1,0:T(8,128)S(1)}, u32[]{:S(2)}, u32[]{:S(2)}) collective-permute-start(f32[128,128]{1,0:T(8,128)S(1)} %convolution_add_fusion.3), channel_id=1, source_target_pairs={{28,0},{0,4},{4,8},{8,12},{12,16},{16,20},{20,24},{24,28},{29,1},{... | collective-permute-start | bytes 196616 | tf_op jit(solution)/shard_map/while/body/eval_jaxpr/ppermute | solution.py:18
  80.4 6.1 %collective-permute-start = (bf16[128,128]{1,0:T(8,128)(2,1)S(1)}, bf16[128,128]{1,0:T(8,128)(2,1)S(1)}, u32[]{:S(2)}, u32[]{:S(2)}) collective-permute-start(bf16[128,128]{1,0:T(8,128)(2,1)S(1)} %copy.30), channel_id=1, source_target_pairs={{28,0},{0,4},{4,8},{8,12},{12,16},{16,20},{20,24},{24,28},{29,1},{... | collective-permute-start | bytes 98312 | tf_op jit(solution)/shard_map/while/body/eval_jaxpr/ppermute | solution.py:18
  80.4 6.1 %collective-permute-start.1 = (bf16[128,128]{1,0:T(8,128)(2,1)S(1)}, bf16[128,128]{1,0:T(8,128)(2,1)S(1)}, u32[]{:S(2)}, u32[]{:S(2)}) collective-permute-start(bf16[128,128]{1,0:T(8,128)(2,1)S(1)} %copy.31), channel_id=1, source_target_pairs={{28,0},{0,4},{4,8},{8,12},{12,16},{16,20},{20,24},{24,28},{29,1},{... | collective-permute-start | bytes 98312 | tf_op jit(solution)/shard_map/while/body/eval_jaxpr/ppermute | solution.py:18
  83.5 4.6 %collective-permute-start.2 = (f32[128,128]{1,0:T(8,128)S(1)}, f32[128,128]{1,0:T(8,128)S(1)}, u32[]{:S(2)}, u32[]{:S(2)}) collective-permute-start(f32[128,128]{1,0:T(8,128)S(1)} %fusion.73), channel_id=1, source_target_pairs={{28,0},{0,4},{4,8},{8,12},{12,16},{16,20},{20,24},{24,28},{29,1},{... | collective-permute-start | bytes 196616 | tf_op jit(solution)/shard_map/while/body/eval_jaxpr/ppermute | solution.py:18
  83.9 5.0 %collective-permute-start.3 = (f32[128,128]{1,0:T(8,128)S(1)}, f32[128,128]{1,0:T(8,128)S(1)}, u32[]{:S(2)}, u32[]{:S(2)}) collective-permute-start(f32[128,128]{1,0:T(8,128)S(1)} %convolution_add_fusion.3), channel_id=1, source_target_pairs={{28,0},{0,4},{4,8},{8,12},{12,16},{16,20},{20,24},{24,28},{29,1},{... | collective-permute-start | bytes 196616 | tf_op jit(solution)/shard_map/while/body/eval_jaxpr/ppermute | solution.py:18
  88.8 7.0 %collective-permute-start.8 = (f32[128,512]{1,0:T(8,128)S(1)}, f32[128,512]{1,0:T(8,128)S(1)}, u32[]{:S(2)}, u32[]{:S(2)}) collective-permute-start(f32[128,512]{1,0:T(8,128)S(1)} %constant_dynamic-slice_fusion), channel_id=1, source_target_pairs={{0,1},{1,0},{2,3},{3,2},{4,5},{5,4},{6,7},{7,6},{8,9},{9,8},{10,11... | collective-permute-start | bytes 786440 | tf_op jit(solution)/shard_map/ppermute | solution.py:12
where the time goes:
time: 97.4 us; the launch traced here: 96.6 us
  starting transfers between devices  30.1 us (31%)
  waiting for transfers between devices  26.9 us (28%)
  matrix products  14 us (14%)
  local copies, waits for them, and re-layouts  13.1 us (13%)
  other arithmetic  10.8 us (11%)
    ppermute x32, starting transfers between devices, shifted(): return lax.ppermute(block, axis, route)  22.9 us
    ppermute x32, waiting for transfers between devices, shifted(): return lax.ppermute(block, axis, route)  21.1 us
    dot_general x24, matrix products, contract_last(): lax.dot_general(left, right, (((1,), (1,)), ((), ())), preferred_element_...  8 us
    ppermute x5, starting transfers between devices, partner(): return lax.ppermute(value, axis, pairs)  7.18 us
    dynamic_slice x9, local copies, waits for them, and re-layouts, slice_meta(): lax.dynamic_slice_in_dim(modality, start, length)  6.85 us
    select_n x16, other arithmetic, local_tile(): same_unit = key_pos[None, :] // UNIT == q_pos[:, None] // UNIT  6.22 us
    ppermute x5, waiting for transfers between devices, partner(): return lax.ppermute(value, axis, pairs)  5.78 us
    dot_general x16, matrix products, contract_first(): lax.dot_general(left, right, (((0,), (0,)), ((), ())), preferred_element_...  4.36 us
  transfers between devices with their start and end apart: 37, of which 19 were waited for; matrix products, arithmetic and copies ran while one was open for 35% of the time, Pallas kernels for 0%

commit v1 on v0

v1 whole, which is shorter than its diff:
```python
import functools

import jax
import jax.numpy as jnp
from jax import lax
from jax.experimental import pallas as pl
from jax.experimental.pallas import tpu as pltpu
from jax.sharding import PartitionSpec as P

UNIT = 64
LOG2E = 1.4426950408889634
MASKED = -1e30
MESH = pl.DeviceIdType.MESH


def contract_first(left, right):
    return lax.dot_general(
        left, right, (((0,), (0,)), ((), ())), preferred_element_type=jnp.float32
    )


def contract_last(left, right):
    return lax.dot_general(
        left, right, (((1,), (1,)), ((), ())), preferred_element_type=jnp.float32
    )


def kernel(
    row_size,
    col_size,
    heads,
    q_ref,
    d_ref,
    o_ref,
    k_ref,
    v_ref,
    lse_ref,
    pos_ref,
    mod_ref,
    table_ref,
    gq_ref,
    gk_ref,
    gv_ref,
    qd,
    aux,
    kv,
    acc,
    out_kv,
    in_kv,
    acc_q,
    out_q,
    in_q,
    kv_send,
    kv_recv,
    qd_send,
    qd_recv,
    grad_send,
    grad_recv,
    q_send,
    q_recv,
):
    me = lax.axis_index("row")
    col = lax.axis_index("col")
    mate = col + 1 - 2 * (col % 2)
    tokens, width = k_ref.shape
    scale = width ** (-0.5)

    def ahead(step):
        return lax.rem(me + step, row_size)

    def behind(step):
        return lax.rem(me - step + row_size, row_size)

    barrier = pltpu.get_barrier_semaphore()

    def greet(step, carry):
        pl.semaphore_signal(barrier, inc=1, device_id={"row": ahead(step)}, device_id_type=MESH)
        return carry

    lax.fori_loop(1, row_size, greet, 0)
    pl.semaphore_signal(barrier, inc=1, device_id={"col": mate}, device_id_type=MESH)

    kv[0, 0] = k_ref[...]
    kv[0, 1] = v_ref[...]
    for h in range(heads):
        lanes = slice(h * width, (h + 1) * width)
        rows = slice(h * tokens, (h + 1) * tokens)
        qd[0, 0, rows, :] = q_ref[:, lanes]
        qd[0, 1, rows, :] = d_ref[:, lanes]
        product = d_ref[:, lanes].astype(jnp.float32) * o_ref[:, lanes].astype(jnp.float32)
        aux[0, heads + h : heads + h + 1, :] = jnp.sum(product.T, axis=0, keepdims=True)
    aux[0, 0:heads, :] = lse_ref[...] * LOG2E

    pl.semaphore_wait(barrier, row_size)

    def kv_copy(step):
        return pltpu.make_async_remote_copy(
            src_ref=kv.at[0],
            dst_ref=kv.at[step],
            send_sem=kv_send.at[step],
            recv_sem=kv_recv.at[step],
            device_id={"row": ahead(step)},
            device_id_type=MESH,
        )

    def grad_copy(step):
        return pltpu.make_async_remote_copy(
            src_ref=out_kv.at[step],
            dst_ref=in_kv.at[step],
            send_sem=grad_send.at[step],
            recv_sem=grad_recv.at[step],
            device_id={"row": behind(step)},
            device_id_type=MESH,
        )

    def to_mate(source, target, send_sem, recv_sem):
        return pltpu.make_async_remote_copy(
            src_ref=source,
            dst_ref=target,
            send_sem=send_sem,
            recv_sem=recv_sem,
            device_id={"col": mate},
            device_id_type=MESH,
        )

    pair_copies = [
        to_mate(qd.at[0], qd.at[1], qd_send.at[0], qd_recv.at[0]),
        to_mate(aux.at[0], aux.at[1], qd_send.at[1], qd_recv.at[1]),
    ]
    q_copy = to_mate(out_q, in_q, q_send, q_recv)

    def send_kv(step, carry):
        kv_copy(step).start()
        return carry

    lax.fori_loop(1, row_size, send_kv, 0)
    for copy in pair_copies:
        copy.start()

    def limits(which_col):
        at = me * col_size + which_col
        pos = pos_ref[pl.ds(at, 1), :]
        mod = mod_ref[pl.ds(at, 1), :]
        last = pos - lax.rem(pos, UNIT) + (UNIT - 1)
        out = []
        for m in range(3):
            seen = jnp.where(
                mod == 0, table_ref[0, m], jnp.where(mod == 1, table_ref[1, m], table_ref[2, m])
            )
            out.append(jnp.where(seen == 1, last, pos))
        return out

    def bias(step, limit):
        at = behind(step) * col_size + col
        shape = (tokens, tokens)
        pos = jnp.broadcast_to(pos_ref[pl.ds(at, 1), :], shape).T
        mod = jnp.broadcast_to(mod_ref[pl.ds(at, 1), :], shape).T
        bound = jnp.where(mod == 0, limit[0], jnp.where(mod == 1, limit[1], limit[2]))
        return jnp.where(pos <= bound, 0.0, MASKED)

    def tile(half, step, limit):
        flat_q = qd[half, 0]
        flat_d = qd[half, 1]
        keys = kv[step, 0]
        values = kv[step, 1]
        lse = jnp.concatenate([aux[half, h : h + 1, :] for h in range(heads)], axis=1)
        delta = jnp.concatenate(
            [aux[half, heads + h : heads + h + 1, :] for h in range(heads)], axis=1
        )
        hidden = jnp.concatenate([bias(step, limit)] * heads, axis=1)
        scores = contract_last(keys, flat_q)
        probs = jnp.exp2(scores * (scale * LOG2E) - lse + hidden)
        grad_probs = contract_last(values, flat_d)
        probs_low = probs.astype(jnp.bfloat16)
        scores_low = (probs * (grad_probs - delta)).astype(jnp.bfloat16)
        grad_v = jnp.dot(probs_low, flat_d, preferred_element_type=jnp.float32)
        grad_k = jnp.dot(scores_low, flat_q, preferred_element_type=jnp.float32)
        grad_q = contract_first(scores_low, keys)
        return grad_q, grad_k, grad_v

    acc_q[...] = jnp.zeros_like(acc_q)
    own_limit = limits(col)
    mate_limit = limits(mate)

    def own_step(step, carry):
        @pl.when(step > 0)
        def _():
            kv_copy(step).wait_recv()

        grad_q, grad_k, grad_v = tile(0, step, own_limit)
        acc_q[0] += grad_q
        acc[step, 0] = grad_k
        acc[step, 1] = grad_v
        return carry

    lax.fori_loop(0, row_size, own_step, 0)

    for copy in pair_copies:
        copy.wait_recv()

    def mate_step(i, carry):
        step = lax.rem(i + 1, row_size)
        grad_q, grad_k, grad_v = tile(1, step, mate_limit)
        acc_q[1] += grad_q
        grad_k = grad_k + acc[step, 0]
        grad_v = grad_v + acc[step, 1]

        @pl.when(step > 0)
        def _():
            out_kv[step, 0] = grad_k.astype(jnp.bfloat16)
            out_kv[step, 1] = grad_v.astype(jnp.bfloat16)
            grad_copy(step).start()

        @pl.when(step == 0)
        def _():
            acc[0, 0] = grad_k
            acc[0, 1] = grad_v

        return carry

    lax.fori_loop(0, row_size, mate_step, 0)

    out_q[...] = acc_q[1].astype(jnp.bfloat16)
    q_copy.start()

    def gather(step, carry):
        grad_copy(step).wait_recv()
        acc[0] += in_kv[step].astype(jnp.float32)
        return carry

    lax.fori_loop(1, row_size, gather, 0)
    gk_ref[...] = (acc[0, 0] * scale).astype(jnp.bfloat16)
    gv_ref[...] = acc[0, 1].astype(jnp.bfloat16)

    q_copy.wait_recv()
    for h in range(heads):
        rows = slice(h * tokens, (h + 1) * tokens)
        total = acc_q[0, rows, :] + in_q[rows, :].astype(jnp.float32)
        gq_ref[:, h * width : (h + 1) * width] = (total * scale).astype(jnp.bfloat16)

    def settle(step, carry):
        kv_copy(step).wait_send()
        grad_copy(step).wait_send()
        return carry

    lax.fori_loop(1, row_size, settle, 0)
    for copy in pair_copies:
        copy.wait_send()
    q_copy.wait_send()


def shards(
    queries,
    grad_out,
    attn_out,
    key_states,
    value_states,
    log_norm,
    position,
    modality,
    bidirectional,
):
    tokens, width = key_states.shape
    heads = log_norm.shape[1]
    row_size = lax.axis_size("row")
    col_size = lax.axis_size("col")
    flat = heads * tokens
    vmem = pl.BlockSpec(memory_space=pltpu.VMEM)
    smem = pl.BlockSpec(memory_space=pltpu.SMEM)
    pairs = row_size * tokens * flat * 2
    return pl.pallas_call(
        functools.partial(kernel, row_size, col_size, heads),
        out_shape=(
            jax.ShapeDtypeStruct(queries.shape, jnp.bfloat16),
            jax.ShapeDtypeStruct(key_states.shape, jnp.bfloat16),
            jax.ShapeDtypeStruct(value_states.shape, jnp.bfloat16),
        ),
        in_specs=[vmem] * 8 + [smem],
        out_specs=(vmem, vmem, vmem),
        scratch_shapes=[
            pltpu.VMEM((2, 2, flat, width), jnp.bfloat16),
            pltpu.VMEM((2, 2 * heads, tokens), jnp.float32),
            pltpu.VMEM((row_size, 2, tokens, width), jnp.bfloat16),
            pltpu.VMEM((row_size, 2, tokens, width), jnp.float32),
            pltpu.VMEM((row_size, 2, tokens, width), jnp.bfloat16),
            pltpu.VMEM((row_size, 2, tokens, width), jnp.bfloat16),
            pltpu.VMEM((2, flat, width), jnp.float32),
            pltpu.VMEM((flat, width), jnp.bfloat16),
            pltpu.VMEM((flat, width), jnp.bfloat16),
            pltpu.SemaphoreType.DMA((row_size,)),
            pltpu.SemaphoreType.DMA((row_size,)),
            pltpu.SemaphoreType.DMA((2,)),
            pltpu.SemaphoreType.DMA((2,)),
            pltpu.SemaphoreType.DMA((row_size,)),
            pltpu.SemaphoreType.DMA((row_size,)),
            pltpu.SemaphoreType.DMA,
            pltpu.SemaphoreType.DMA,
        ],
        compiler_params=pltpu.CompilerParams(
            collective_id=0, has_side_effects=True, vmem_limit_bytes=40 * 2**20
        ),
        cost_estimate=pl.CostEstimate(
            flops=10 * pairs * width, bytes_accessed=8 * flat * width, transcendentals=pairs
        ),
    )(
        queries,
        grad_out,
        attn_out,
        key_states,
        value_states,
        log_norm.T,
        position.reshape(-1, tokens),
        modality.reshape(-1, tokens),
        bidirectional,
    )


def solution(mesh):
    split = P(("row", "col"), None)
    return jax.shard_map(
        shards,
        mesh=mesh,
        in_specs=(split,) * 6 + (P(), P(), P()),
        out_specs=(split, split, split),
        check_vma=False,
    )
```

time: 97.4 us -> 32.4 us (0.33)
  starting transfers between devices: 30.1 us -> 0 us
  waiting for transfers between devices: 26.9 us -> 0 us
  Pallas kernels: 0 us -> 23.1 us
  matrix products: 14 us -> 0 us
  other arithmetic: 10.8 us -> 0 us
  local copies, waits for them, and re-layouts: 13.1 us -> 8.23 us
    ppermute x37 -> x0, starting transfers between devices: 30.1 us -> none  [the longest x32 22.9 us: shifted(): return lax.ppermute(block, axis, route)]
    ppermute x37 -> x0, waiting for transfers between devices: 26.9 us -> none  [the longest x32 21.1 us: shifted(): return lax.ppermute(block, axis, route)]
    pallas_call x0 -> x1, Pallas kernels: none -> 23.1 us  [shards(): pl.pallas_call(functools.partial(kernel, row_size, col_size, heads), out_...]
    dot_general x48 -> x0, matrix products: 14 us -> none  [the longest x24 8 us: contract_last(): lax.dot_general(left, right, (((1,), (1,)), ((), ())), preferred_element_...]
    dynamic_slice x10 -> x0, local copies, waits for them, and re-layouts: 6.87 us -> none  [the longest x9 6.85 us: slice_meta(): lax.dynamic_slice_in_dim(modality, start, length)]
    select_n x19 -> x0, other arithmetic: 6.27 us -> none  [the longest x16 6.22 us: local_tile(): same_unit = key_pos[None, :] // UNIT == q_pos[:, None] // UNIT]
    unnamed x24 -> x21, local copies, waits for them, and re-layouts: 2.94 us -> 8.23 us
    reshape x12 -> x0, local copies, waits for them, and re-layouts: 1.98 us -> none  [the longest x1 0.97 us: shards(): grad_out.reshape(tok_count, head_count, head_width)]
  transfers between devices with their start and end apart: 37 -> 0, of which waited for: 19 -> 0; matrix products, arithmetic and copies ran while one was open for 35% -> 0% of each run, Pallas kernels for 0% -> 0%
where the time goes in v1:
time: 32.4 us; the launch traced here: 32 us
  Pallas kernels  23.1 us (71%)
  local copies, waits for them, and re-layouts  8.23 us (25%)
  between operations  0.67 us (2%)
    pallas_call x1, Pallas kernels, shards(): pl.pallas_call(functools.partial(kernel, row_size, col_size, heads), out_...  23.1 us
    unnamed x21, local copies, waits for them, and re-layouts  8.23 us

profile of v1, /device:TPU:0, one launch (start us, length us, event | category | flops | bytes accessed | tf_op | source)
XLA Modules:
  0.0 32.0 jit_solution(1918014118736049565)
XLA Ops:
  0.6 0.0 copy-start.8
  0.6 0.0 copy-start.7
  0.7 0.7 %copy-done.8 = s32[3,3]{1,0:T(4,128)S(1)} copy-done((s32[3,3]{1,0:T(4,128)S(1)}, s32[3,3]{1,0:T(4,128)}, u32[]{:S(2)}) %copy-start.8) | copy-done | bytes 60
  1.3 0.0 copy-done.7
  1.3 0.0 copy-start
  1.3 0.9 %copy-done = bf16[128,512]{1,0:T(8,128)(2,1)S(1)} copy-done((bf16[128,512]{1,0:T(8,128)(2,1)S(1)}, bf16[128,512]{1,0:T(8,128)(2,1)}, u32[]{:S(2)}) %copy-start) | copy-done | bytes 131096
  2.2 0.0 copy-start.1
  2.2 0.9 %copy-done.1 = bf16[128,512]{1,0:T(8,128)(2,1)S(1)} copy-done((bf16[128,512]{1,0:T(8,128)(2,1)S(1)}, bf16[128,512]{1,0:T(8,128)(2,1)}, u32[]{:S(2)}) %copy-start.1) | copy-done | bytes 131096
  3.1 0.0 copy-start.2
  3.1 0.9 %copy-done.2 = bf16[128,512]{1,0:T(8,128)(2,1)S(1)} copy-done((bf16[128,512]{1,0:T(8,128)(2,1)S(1)}, bf16[128,512]{1,0:T(8,128)(2,1)}, u32[]{:S(2)}) %copy-start.2) | copy-done | bytes 131096
  4.0 0.0 copy-start.3
  4.0 0.8 %copy-done.3 = bf16[128,128]{1,0:T(8,128)(2,1)S(1)} copy-done((bf16[128,128]{1,0:T(8,128)(2,1)S(1)}, bf16[128,128]{1,0:T(8,128)(2,1)}, u32[]{:S(2)}) %copy-start.3) | copy-done | bytes 32792
  4.8 0.0 copy-start.4
  4.8 0.8 %copy-done.4 = bf16[128,128]{1,0:T(8,128)(2,1)S(1)} copy-done((bf16[128,128]{1,0:T(8,128)(2,1)S(1)}, bf16[128,128]{1,0:T(8,128)(2,1)}, u32[]{:S(2)}) %copy-start.4) | copy-done | bytes 32792
  5.6 0.0 copy-start.5
  5.6 0.7 %copy-done.5 = s32[4096]{0:T(1024)S(1)} copy-done((s32[4096]{0:T(1024)S(1)}, s32[4096]{0:T(1024)}, u32[]{:S(2)}) %copy-start.5) | copy-done | bytes 16408
  6.3 0.0 copy-start.6
  6.3 0.7 %copy-done.6 = s32[4096]{0:T(1024)S(1)} copy-done((s32[4096]{0:T(1024)S(1)}, s32[4096]{0:T(1024)}, u32[]{:S(2)}) %copy-start.6) | copy-done | bytes 16408
  7.0 23.1 %shard_map.112 = (bf16[128,512]{1,0:T(8,128)(2,1)S(1)}, bf16[128,128]{1,0:T(8,128)(2,1)S(1)}, bf16[128,128]{1,0:T(8,128)(2,1)S(1)}) custom-call(bf16[128,512]{1,0:T(8,128)(2,1)S(1)} %copy-done, bf16[128,512]{1,0:T(8,128)(2,1)S(1)} %copy-done.1, bf16[128,512]{1,0:T(8,128)(2,1)S(1)} %copy-done.2, bf16[128,128]{1,0:T(8,128)(2,1)S(1)} %copy-done.3, ...), custom_call_target="tpu_custom_call" | custom-call | flops 1342177280 | bytes 524288 | tf_op jit(solution)/shard_map/pallas_call | solution.py:271
  30.1 0.7 %copy.15 = bf16[128,512]{1,0:T(8,128)(2,1)} copy(bf16[128,512]{1,0:T(8,128)(2,1)S(1)} %get-tuple-element.6) | data formatting | bytes 262144
  30.8 0.6 %copy.16 = bf16[128,128]{1,0:T(8,128)(2,1)} copy(bf16[128,128]{1,0:T(8,128)(2,1)S(1)} %get-tuple-element.7) | data formatting | bytes 65536
  31.4 0.6 %copy.17 = bf16[128,128]{1,0:T(8,128)(2,1)} copy(bf16[128,128]{1,0:T(8,128)(2,1)S(1)} %get-tuple-element.8) | data formatting | bytes 65536
Async XLA Ops:
  0.6 0.7 %copy-start.8 = (s32[3,3]{1,0:T(4,128)S(1)}, s32[3,3]{1,0:T(4,128)}, u32[]{:S(2)}) copy-start(s32[3,3]{1,0:T(4,128)} %table_ref.1) | copy-start | bytes 112
  0.6 0.7 %copy-start.7 = (f32[128,4]{0,1:T(4,128)S(1)}, f32[128,4]{0,1:T(4,128)}, u32[]{:S(2)}) copy-start(f32[128,4]{0,1:T(4,128)} %param.14) | copy-start | bytes 6148
  1.3 0.9 %copy-start = (bf16[128,512]{1,0:T(8,128)(2,1)S(1)}, bf16[128,512]{1,0:T(8,128)(2,1)}, u32[]{:S(2)}) copy-start(bf16[128,512]{1,0:T(8,128)(2,1)} %q_ref.1) | copy-start | bytes 393220
  2.2 0.9 %copy-start.1 = (bf16[128,512]{1,0:T(8,128)(2,1)S(1)}, bf16[128,512]{1,0:T(8,128)(2,1)}, u32[]{:S(2)}) copy-start(bf16[128,512]{1,0:T(8,128)(2,1)} %d_ref.1) | copy-start | bytes 393220
  3.1 0.9 %copy-start.2 = (bf16[128,512]{1,0:T(8,128)(2,1)S(1)}, bf16[128,512]{1,0:T(8,128)(2,1)}, u32[]{:S(2)}) copy-start(bf16[128,512]{1,0:T(8,128)(2,1)} %o_ref.1) | copy-start | bytes 393220
  4.0 0.8 %copy-start.3 = (bf16[128,128]{1,0:T(8,128)(2,1)S(1)}, bf16[128,128]{1,0:T(8,128)(2,1)}, u32[]{:S(2)}) copy-start(bf16[128,128]{1,0:T(8,128)(2,1)} %k_ref.1) | copy-start | bytes 98308
  4.8 0.8 %copy-start.4 = (bf16[128,128]{1,0:T(8,128)(2,1)S(1)}, bf16[128,128]{1,0:T(8,128)(2,1)}, u32[]{:S(2)}) copy-start(bf16[128,128]{1,0:T(8,128)(2,1)} %v_ref.1) | copy-start | bytes 98308
  5.6 0.7 %copy-start.5 = (s32[4096]{0:T(1024)S(1)}, s32[4096]{0:T(1024)}, u32[]{:S(2)}) copy-start(s32[4096]{0:T(1024)} %param.15) | copy-start | bytes 49156
  6.3 0.7 %copy-start.6 = (s32[4096]{0:T(1024)S(1)}, s32[4096]{0:T(1024)}, u32[]{:S(2)}) copy-start(s32[4096]{0:T(1024)} %param.16) | copy-start | bytes 49156

commit v2 on v1

--- a/solution.py
+++ b/solution.py
@@ -29,15 +29,15 @@
     row_size,
     col_size,
     heads,
-    q_ref,
-    d_ref,
-    o_ref,
-    k_ref,
-    v_ref,
-    lse_ref,
-    pos_ref,
-    mod_ref,
-    table_ref,
+    q_hbm,
+    d_hbm,
+    o_hbm,
+    k_hbm,
+    v_hbm,
+    lse_hbm,
+    pos_hbm,
+    mod_hbm,
+    table_hbm,
     gq_ref,
     gk_ref,
     gv_ref,
@@ -58,11 +58,17 @@
     grad_recv,
     q_send,
     q_recv,
+    o_ref,
+    lse_ref,
+    pos_ref,
+    mod_ref,
+    table_ref,
+    load,
 ):
     me = lax.axis_index("row")
     col = lax.axis_index("col")
     mate = col + 1 - 2 * (col % 2)
-    tokens, width = k_ref.shape
+    tokens, width = k_hbm.shape
     scale = width ** (-0.5)
 
     def ahead(step):
@@ -71,6 +77,26 @@
     def behind(step):
         return lax.rem(me - step + row_size, row_size)
 
+    sources = [(k_hbm, kv.at[0, 0]), (v_hbm, kv.at[0, 1])]
+    for array, stacked in ((q_hbm, qd.at[0, 0]), (d_hbm, qd.at[0, 1]), (o_hbm, o_ref)):
+        for h in range(heads):
+            lanes = slice(h * width, (h + 1) * width)
+            rows = slice(h * tokens, (h + 1) * tokens)
+            sources.append((array.at[:, lanes], stacked.at[rows, :]))
+    sources += [
+        (lse_hbm, lse_ref),
+        (pos_hbm, pos_ref),
+        (mod_hbm, mod_ref),
+        (table_hbm, table_ref),
+    ]
+    loads = [
+        pltpu.make_async_copy(source, target, load.at[i])
+        for i, (source, target) in enumerate(sources)
+    ]
+    for copy in loads:
+        copy.start()
+    kv_loads, qd_loads, other_loads = loads[:2], loads[2 : 2 + 2 * heads], loads[2 + 2 * heads :]
+
     barrier = pltpu.get_barrier_semaphore()
 
     def greet(step, carry):
@@ -79,19 +105,6 @@
 
     lax.fori_loop(1, row_size, greet, 0)
     pl.semaphore_signal(barrier, inc=1, device_id={"col": mate}, device_id_type=MESH)
-
-    kv[0, 0] = k_ref[...]
-    kv[0, 1] = v_ref[...]
-    for h in range(heads):
-        lanes = slice(h * width, (h + 1) * width)
-        rows = slice(h * tokens, (h + 1) * tokens)
-        qd[0, 0, rows, :] = q_ref[:, lanes]
-        qd[0, 1, rows, :] = d_ref[:, lanes]
-        product = d_ref[:, lanes].astype(jnp.float32) * o_ref[:, lanes].astype(jnp.float32)
-        aux[0, heads + h : heads + h + 1, :] = jnp.sum(product.T, axis=0, keepdims=True)
-    aux[0, 0:heads, :] = lse_ref[...] * LOG2E
-
-    pl.semaphore_wait(barrier, row_size)
 
     def kv_copy(step):
         return pltpu.make_async_remote_copy(
@@ -133,9 +146,21 @@
         kv_copy(step).start()
         return carry
 
+    for copy in kv_loads:
+        copy.wait()
+    pl.semaphore_wait(barrier, row_size)
     lax.fori_loop(1, row_size, send_kv, 0)
-    for copy in pair_copies:
-        copy.start()
+    for copy in qd_loads:
+        copy.wait()
+    pair_copies[0].start()
+    for copy in other_loads:
+        copy.wait()
+    for h in range(heads):
+        rows = slice(h * tokens, (h + 1) * tokens)
+        product = qd[0, 1, rows, :].astype(jnp.float32) * o_ref[rows, :].astype(jnp.float32)
+        aux[0, heads + h : heads + h + 1, :] = jnp.sum(product.T, axis=0, keepdims=True)
+    aux[0, 0:heads, :] = lse_ref[...] * LOG2E
+    pair_copies[1].start()
 
     def limits(which_col):
         at = me * col_size + which_col
@@ -144,9 +169,8 @@
         last = pos - lax.rem(pos, UNIT) + (UNIT - 1)
         out = []
         for m in range(3):
-            seen = jnp.where(
-                mod == 0, table_ref[0, m], jnp.where(mod == 1, table_ref[1, m], table_ref[2, m])
-            )
+            from_text, from_image, from_video = (table_ref[a : a + 1, m : m + 1] for a in range(3))
+            seen = jnp.where(mod == 0, from_text, jnp.where(mod == 1, from_image, from_video))
             out.append(jnp.where(seen == 1, last, pos))
         return out
 
@@ -249,6 +273,18 @@
     q_copy.wait_send()
 
 
+def write_out(gq_ref, gk_ref, gv_ref, gq_hbm, gk_hbm, gv_hbm, sems):
+    copies = [
+        pltpu.make_async_copy(gq_ref, gq_hbm, sems.at[0]),
+        pltpu.make_async_copy(gk_ref, gk_hbm, sems.at[1]),
+        pltpu.make_async_copy(gv_ref, gv_hbm, sems.at[2]),
+    ]
+    for copy in copies:
+        copy.start()
+    for copy in copies:
+        copy.wait()
+
+
 def shards(
     queries,
     grad_out,
@@ -266,16 +302,18 @@
     col_size = lax.axis_size("col")
     flat = heads * tokens
     vmem = pl.BlockSpec(memory_space=pltpu.VMEM)
-    smem = pl.BlockSpec(memory_space=pltpu.SMEM)
+    hbm = pl.BlockSpec(memory_space=pltpu.HBM)
     pairs = row_size * tokens * flat * 2
-    return pl.pallas_call(
+    out_shape = (
+        jax.ShapeDtypeStruct(queries.shape, jnp.bfloat16),
+        jax.ShapeDtypeStruct(key_states.shape, jnp.bfloat16),
+        jax.ShapeDtypeStruct(value_states.shape, jnp.bfloat16),
+    )
+    positions = position.reshape(-1, tokens)
+    grads = pl.pallas_call(
         functools.partial(kernel, row_size, col_size, heads),
-        out_shape=(
-            jax.ShapeDtypeStruct(queries.shape, jnp.bfloat16),
-            jax.ShapeDtypeStruct(key_states.shape, jnp.bfloat16),
-            jax.ShapeDtypeStruct(value_states.shape, jnp.bfloat16),
-        ),
-        in_specs=[vmem] * 8 + [smem],
+        out_shape=out_shape,
+        in_specs=[hbm] * 9,
         out_specs=(vmem, vmem, vmem),
         scratch_shapes=[
             pltpu.VMEM((2, 2, flat, width), jnp.bfloat16),
@@ -295,6 +333,12 @@
             pltpu.SemaphoreType.DMA((row_size,)),
             pltpu.SemaphoreType.DMA,
             pltpu.SemaphoreType.DMA,
+            pltpu.VMEM((flat, width), jnp.bfloat16),
+            pltpu.VMEM((heads, tokens), jnp.float32),
+            pltpu.VMEM(positions.shape, jnp.int32),
+            pltpu.VMEM(positions.shape, jnp.int32),
+            pltpu.VMEM(bidirectional.shape, jnp.int32),
+            pltpu.SemaphoreType.DMA((3 * heads + 6,)),
         ],
         compiler_params=pltpu.CompilerParams(
             collective_id=0, has_side_effects=True, vmem_limit_bytes=40 * 2**20
@@ -302,17 +346,25 @@
         cost_estimate=pl.CostEstimate(
             flops=10 * pairs * width, bytes_accessed=8 * flat * width, transcendentals=pairs
         ),
-    )(
+    )(*(pltpu.with_memory_space_constraint(x, pltpu.HBM) for x in (
         queries,
         grad_out,
         attn_out,
         key_states,
         value_states,
         log_norm.T,
-        position.reshape(-1, tokens),
+        positions,
         modality.reshape(-1, tokens),
         bidirectional,
-    )
+    )))
+    return pl.pallas_call(
+        write_out,
+        out_shape=out_shape,
+        in_specs=[pl.BlockSpec(memory_space=pl.ANY)] * 3,
+        out_specs=(hbm, hbm, hbm),
+        scratch_shapes=[pltpu.SemaphoreType.DMA((3,))],
+        compiler_params=pltpu.CompilerParams(vmem_limit_bytes=2**20),
+    )(*grads)
 
 
 def solution(mesh):

time: 32.4 us -> 24.3 us (0.75)
  local copies, waits for them, and re-layouts: 8.23 us -> 0 us
    unnamed x21 -> x0, local copies, waits for them, and re-layouts: 8.23 us -> none
    pallas_call x0 -> x1, Pallas kernels: none -> 0.7 us  [shards(): pl.pallas_call(write_out, out_shape=out_shape, in_specs=[pl.BlockSpec(mem...]
    pallas_call x1, Pallas kernels: 23.1 us -> 22.7 us  [shards(): pl.pallas_call(functools.partial(kernel, row_size, col_size, heads), out_...]
where the time goes in v2:
time: 24.3 us; the launch traced here: 24.1 us
  Pallas kernels  23.4 us (96%)
  between operations  0.64 us (3%)
    pallas_call x1, Pallas kernels, shards(): pl.pallas_call(functools.partial(kernel, row_size, col_size, heads), out_...  22.7 us
    pallas_call x1, Pallas kernels, shards(): pl.pallas_call(write_out, out_shape=out_shape, in_specs=[pl.BlockSpec(mem...  0.7 us

profile of v2, /device:TPU:0, one launch (start us, length us, event | category | flops | bytes accessed | tf_op | source)
XLA Modules:
  0.0 24.1 jit_solution(1395721995943491699)
XLA Ops:
  0.6 22.7 %shard_map.112 = (bf16[128,512]{1,0:T(8,128)(2,1)S(1)}, bf16[128,128]{1,0:T(8,128)(2,1)S(1)}, bf16[128,128]{1,0:T(8,128)(2,1)S(1)}) custom-call(bf16[128,512]{1,0:T(8,128)(2,1)} %q_hbm.1, bf16[128,512]{1,0:T(8,128)(2,1)} %d_hbm.1, bf16[128,512]{1,0:T(8,128)(2,1)} %o_hbm.1, bf16[128,128]{1,0:T(8,128)(2,1)} %k_hbm.1, bf16[128,128]{1,0:T(8,128)(2,1)} %v_hbm.1, ...), custom_call_target="tpu_custom_call" | custom-call | flops 1342177280 | bytes 524288 | tf_op jit(solution)/shard_map/pallas_call | solution.py:313
  23.4 0.7 %shard_map.113 = (bf16[128,512]{1,0:T(8,128)(2,1)}, bf16[128,128]{1,0:T(8,128)(2,1)}, bf16[128,128]{1,0:T(8,128)(2,1)}) custom-call(bf16[128,512]{1,0:T(8,128)(2,1)S(1)} %get-tuple-element.6.gq_ref, bf16[128,128]{1,0:T(8,128)(2,1)S(1)} %get-tuple-element.7.gk_ref, bf16[128,128]{1,0:T(8,128)(2,1)S(1)} %get-tuple-element.8.gv_ref), custom_call_target="tpu_custom_call" | custom-call | tf_op jit(solution)/shard_map/pallas_call | solution.py:360

commit v3 on v2

--- a/solution.py
+++ b/solution.py
@@ -45,6 +45,8 @@
     aux,
     kv,
     acc,
+    out_sib,
+    in_sib,
     out_kv,
     in_kv,
     acc_q,
@@ -52,6 +54,8 @@
     in_q,
     kv_send,
     kv_recv,
+    sib_send,
+    sib_recv,
     qd_send,
     qd_recv,
     grad_send,
@@ -71,11 +75,15 @@
     tokens, width = k_hbm.shape
     scale = width ** (-0.5)
 
-    def ahead(step):
-        return lax.rem(me + step, row_size)
-
-    def behind(step):
-        return lax.rem(me - step + row_size, row_size)
+    chips = row_size // 2
+    chip, core = me // 2, lax.rem(me, 2)
+    sibling = 2 * chip + 1 - core
+
+    def ahead(c):
+        return 2 * lax.rem(chip + c, chips) + core
+
+    def behind(c, other=0):
+        return 2 * lax.rem(chip - c + chips, chips) + (1 - core if other else core)
 
     sources = [(k_hbm, kv.at[0, 0]), (v_hbm, kv.at[0, 1])]
     for array, stacked in ((q_hbm, qd.at[0, 0]), (d_hbm, qd.at[0, 1]), (o_hbm, o_ref)):
@@ -103,28 +111,33 @@
         pl.semaphore_signal(barrier, inc=1, device_id={"row": ahead(step)}, device_id_type=MESH)
         return carry
 
-    lax.fori_loop(1, row_size, greet, 0)
+    lax.fori_loop(1, chips, greet, 0)
+    pl.semaphore_signal(barrier, inc=1, device_id={"row": sibling}, device_id_type=MESH)
     pl.semaphore_signal(barrier, inc=1, device_id={"col": mate}, device_id_type=MESH)
 
-    def kv_copy(step):
+    def remote(source, target, send_sem, recv_sem, row):
         return pltpu.make_async_remote_copy(
-            src_ref=kv.at[0],
-            dst_ref=kv.at[step],
-            send_sem=kv_send.at[step],
-            recv_sem=kv_recv.at[step],
-            device_id={"row": ahead(step)},
+            src_ref=source,
+            dst_ref=target,
+            send_sem=send_sem,
+            recv_sem=recv_sem,
+            device_id={"row": row},
             device_id_type=MESH,
         )
 
-    def grad_copy(step):
-        return pltpu.make_async_remote_copy(
-            src_ref=out_kv.at[step],
-            dst_ref=in_kv.at[step],
-            send_sem=grad_send.at[step],
-            recv_sem=grad_recv.at[step],
-            device_id={"row": behind(step)},
-            device_id_type=MESH,
-        )
+    def kv_copy(c):
+        slot = 2 * c
+        return remote(kv.at[0], kv.at[slot], kv_send.at[slot], kv_recv.at[slot], ahead(c))
+
+    def kv_share(c):
+        slot = 2 * c + 1
+        return remote(kv.at[2 * c], kv.at[slot], kv_send.at[slot], kv_recv.at[slot], sibling)
+
+    def grad_share(c):
+        return remote(out_sib.at[c], in_sib.at[c], sib_send.at[c], sib_recv.at[c], sibling)
+
+    def grad_copy(c):
+        return remote(out_kv.at[c], in_kv.at[c], grad_send.at[c], grad_recv.at[c], behind(c))
 
     def to_mate(source, target, send_sem, recv_sem):
         return pltpu.make_async_remote_copy(
@@ -148,8 +161,9 @@
 
     for copy in kv_loads:
         copy.wait()
-    pl.semaphore_wait(barrier, row_size)
-    lax.fori_loop(1, row_size, send_kv, 0)
+    pl.semaphore_wait(barrier, chips + 1)
+    kv_share(0).start()
+    lax.fori_loop(1, chips, send_kv, 0)
     for copy in qd_loads:
         copy.wait()
     pair_copies[0].start()
@@ -174,24 +188,25 @@
             out.append(jnp.where(seen == 1, last, pos))
         return out
 
-    def bias(step, limit):
-        at = behind(step) * col_size + col
+    def bias(c, other, limit):
+        at = behind(c, other) * col_size + col
         shape = (tokens, tokens)
         pos = jnp.broadcast_to(pos_ref[pl.ds(at, 1), :], shape).T
         mod = jnp.broadcast_to(mod_ref[pl.ds(at, 1), :], shape).T
         bound = jnp.where(mod == 0, limit[0], jnp.where(mod == 1, limit[1], limit[2]))
         return jnp.where(pos <= bound, 0.0, MASKED)
 
-    def tile(half, step, limit):
+    def tile(half, c, limit):
         flat_q = qd[half, 0]
         flat_d = qd[half, 1]
-        keys = kv[step, 0]
-        values = kv[step, 1]
+        keys = kv[pl.ds(2 * c, 2), 0].reshape(2 * tokens, width)
+        values = kv[pl.ds(2 * c, 2), 1].reshape(2 * tokens, width)
         lse = jnp.concatenate([aux[half, h : h + 1, :] for h in range(heads)], axis=1)
         delta = jnp.concatenate(
             [aux[half, heads + h : heads + h + 1, :] for h in range(heads)], axis=1
         )
-        hidden = jnp.concatenate([bias(step, limit)] * heads, axis=1)
+        hidden = jnp.concatenate([bias(c, 0, limit), bias(c, 1, limit)], axis=0)
+        hidden = jnp.concatenate([hidden] * heads, axis=1)
         scores = contract_last(keys, flat_q)
         probs = jnp.exp2(scores * (scale * LOG2E) - lse + hidden)
         grad_probs = contract_last(values, flat_d)
@@ -206,53 +221,59 @@
     own_limit = limits(col)
     mate_limit = limits(mate)
 
-    def own_step(step, carry):
-        @pl.when(step > 0)
-        def _():
-            kv_copy(step).wait_recv()
-
-        grad_q, grad_k, grad_v = tile(0, step, own_limit)
+    def own_step(c, carry):
+        kv_share(c).wait_recv()
+        grad_q, grad_k, grad_v = tile(0, c, own_limit)
         acc_q[0] += grad_q
-        acc[step, 0] = grad_k
-        acc[step, 1] = grad_v
-        return carry
-
-    lax.fori_loop(0, row_size, own_step, 0)
+        for e in range(2):
+            rows = slice(e * tokens, (e + 1) * tokens)
+            acc[2 * c + e, 0] = grad_k[rows]
+            acc[2 * c + e, 1] = grad_v[rows]
+        return carry
+
+    def share_kv(c, carry):
+        kv_copy(c).wait_recv()
+        kv_share(c).start()
+        return carry
+
+    lax.fori_loop(1, chips, share_kv, 0)
+    lax.fori_loop(0, chips, own_step, 0)
 
     for copy in pair_copies:
         copy.wait_recv()
 
     def mate_step(i, carry):
-        step = lax.rem(i + 1, row_size)
-        grad_q, grad_k, grad_v = tile(1, step, mate_limit)
+        c = lax.rem(i + 1, chips)
+        grad_q, grad_k, grad_v = tile(1, c, mate_limit)
         acc_q[1] += grad_q
-        grad_k = grad_k + acc[step, 0]
-        grad_v = grad_v + acc[step, 1]
-
-        @pl.when(step > 0)
+        acc[2 * c, 0] += grad_k[:tokens]
+        acc[2 * c, 1] += grad_v[:tokens]
+        out_sib[c, 0] = (grad_k[tokens:] + acc[2 * c + 1, 0]).astype(jnp.bfloat16)
+        out_sib[c, 1] = (grad_v[tokens:] + acc[2 * c + 1, 1]).astype(jnp.bfloat16)
+        grad_share(c).start()
+
+        @pl.when(i > 0)
         def _():
-            out_kv[step, 0] = grad_k.astype(jnp.bfloat16)
-            out_kv[step, 1] = grad_v.astype(jnp.bfloat16)
-            grad_copy(step).start()
-
-        @pl.when(step == 0)
-        def _():
-            acc[0, 0] = grad_k
-            acc[0, 1] = grad_v
-
-        return carry
-
-    lax.fori_loop(0, row_size, mate_step, 0)
+            grad_share(i).wait_recv()
+            total = acc[2 * i] + in_sib[i].astype(jnp.float32)
+            out_kv[i] = total.astype(jnp.bfloat16)
+            grad_copy(i).start()
+
+        return carry
+
+    lax.fori_loop(0, chips, mate_step, 0)
 
     out_q[...] = acc_q[1].astype(jnp.bfloat16)
     q_copy.start()
 
-    def gather(step, carry):
-        grad_copy(step).wait_recv()
-        acc[0] += in_kv[step].astype(jnp.float32)
-        return carry
-
-    lax.fori_loop(1, row_size, gather, 0)
+    def gather(c, carry):
+        grad_copy(c).wait_recv()
+        acc[0] += in_kv[c].astype(jnp.float32)
+        return carry
+
+    grad_share(0).wait_recv()
+    acc[0] += in_sib[0].astype(jnp.float32)
+    lax.fori_loop(1, chips, gather, 0)
     gk_ref[...] = (acc[0, 0] * scale).astype(jnp.bfloat16)
     gv_ref[...] = acc[0, 1].astype(jnp.bfloat16)
 
@@ -264,10 +285,14 @@
 
     def settle(step, carry):
         kv_copy(step).wait_send()
+        kv_share(step).wait_send()
         grad_copy(step).wait_send()
-        return carry
-
-    lax.fori_loop(1, row_size, settle, 0)
+        grad_share(step).wait_send()
+        return carry
+
+    kv_share(0).wait_send()
+    grad_share(0).wait_send()
+    lax.fori_loop(1, chips, settle, 0)
     for copy in pair_copies:
         copy.wait_send()
     q_copy.wait_send()
@@ -301,6 +326,7 @@
     row_size = lax.axis_size("row")
     col_size = lax.axis_size("col")
     flat = heads * tokens
+    chips = row_size // 2
     vmem = pl.BlockSpec(memory_space=pltpu.VMEM)
     hbm = pl.BlockSpec(memory_space=pltpu.HBM)
     pairs = row_size * tokens * flat * 2
@@ -320,17 +346,21 @@
             pltpu.VMEM((2, 2 * heads, tokens), jnp.float32),
             pltpu.VMEM((row_size, 2, tokens, width), jnp.bfloat16),
             pltpu.VMEM((row_size, 2, tokens, width), jnp.float32),
-            pltpu.VMEM((row_size, 2, tokens, width), jnp.bfloat16),
-            pltpu.VMEM((row_size, 2, tokens, width), jnp.bfloat16),
+            pltpu.VMEM((chips, 2, tokens, width), jnp.bfloat16),
+            pltpu.VMEM((chips, 2, tokens, width), jnp.bfloat16),
+            pltpu.VMEM((chips, 2, tokens, width), jnp.bfloat16),
+            pltpu.VMEM((chips, 2, tokens, width), jnp.bfloat16),
             pltpu.VMEM((2, flat, width), jnp.float32),
             pltpu.VMEM((flat, width), jnp.bfloat16),
             pltpu.VMEM((flat, width), jnp.bfloat16),
             pltpu.SemaphoreType.DMA((row_size,)),
             pltpu.SemaphoreType.DMA((row_size,)),
+            pltpu.SemaphoreType.DMA((chips,)),
+            pltpu.SemaphoreType.DMA((chips,)),
             pltpu.SemaphoreType.DMA((2,)),
             pltpu.SemaphoreType.DMA((2,)),
-            pltpu.SemaphoreType.DMA((row_size,)),
-            pltpu.SemaphoreType.DMA((row_size,)),
+            pltpu.SemaphoreType.DMA((chips,)),
+            pltpu.SemaphoreType.DMA((chips,)),
             pltpu.SemaphoreType.DMA,
             pltpu.SemaphoreType.DMA,
             pltpu.VMEM((flat, width), jnp.bfloat16),

time: 24.3 us -> 21.1 us (0.87)
  Pallas kernels: 23.4 us -> 20.3 us
    pallas_call x1, Pallas kernels: 22.7 us -> 19.6 us  [shards(): pl.pallas_call(functools.partial(kernel, row_size, col_size, heads), out_...]
where the time goes in v3:
time: 21.1 us; the launch traced here: 21 us
  Pallas kernels  20.3 us (96%)
  between operations  0.64 us (3%)
    pallas_call x1, Pallas kernels, shards(): pl.pallas_call(functools.partial(kernel, row_size, col_size, heads), out_...  19.6 us
    pallas_call x1, Pallas kernels, shards(): pl.pallas_call(write_out, out_shape=out_shape, in_specs=[pl.BlockSpec(mem...  0.7 us

profile of v3, /device:TPU:0, one launch (start us, length us, event | category | flops | bytes accessed | tf_op | source)
XLA Modules:
  0.0 21.0 jit_solution(18114590790046606270)
XLA Ops:
  0.6 19.6 %shard_map.112 = (bf16[128,512]{1,0:T(8,128)(2,1)S(1)}, bf16[128,128]{1,0:T(8,128)(2,1)S(1)}, bf16[128,128]{1,0:T(8,128)(2,1)S(1)}) custom-call(bf16[128,512]{1,0:T(8,128)(2,1)} %q_hbm.1, bf16[128,512]{1,0:T(8,128)(2,1)} %d_hbm.1, bf16[128,512]{1,0:T(8,128)(2,1)} %o_hbm.1, bf16[128,128]{1,0:T(8,128)(2,1)} %k_hbm.1, bf16[128,128]{1,0:T(8,128)(2,1)} %v_hbm.1, ...), custom_call_target="tpu_custom_call" | custom-call | flops 1342177280 | bytes 524288 | tf_op jit(solution)/shard_map/pallas_call | solution.py:339
  20.3 0.7 %shard_map.113 = (bf16[128,512]{1,0:T(8,128)(2,1)}, bf16[128,128]{1,0:T(8,128)(2,1)}, bf16[128,128]{1,0:T(8,128)(2,1)}) custom-call(bf16[128,512]{1,0:T(8,128)(2,1)S(1)} %get-tuple-element.6.gq_ref, bf16[128,128]{1,0:T(8,128)(2,1)S(1)} %get-tuple-element.7.gk_ref, bf16[128,128]{1,0:T(8,128)(2,1)S(1)} %get-tuple-element.8.gv_ref), custom_call_target="tpu_custom_call" | custom-call | tf_op jit(solution)/shard_map/pallas_call | solution.py:390

commit v4 on v3

--- a/solution.py
+++ b/solution.py
@@ -236,11 +236,18 @@
         kv_share(c).start()
         return carry
 
+    own_step(0, 0)
     lax.fori_loop(1, chips, share_kv, 0)
-    lax.fori_loop(0, chips, own_step, 0)
+    lax.fori_loop(1, chips, own_step, 0)
 
     for copy in pair_copies:
         copy.wait_recv()
+
+    def pass_on(c):
+        grad_share(c).wait_recv()
+        total = acc[2 * c] + in_sib[c].astype(jnp.float32)
+        out_kv[c] = total.astype(jnp.bfloat16)
+        grad_copy(c).start()
 
     def mate_step(i, carry):
         c = lax.rem(i + 1, chips)
@@ -252,12 +259,9 @@
         out_sib[c, 1] = (grad_v[tokens:] + acc[2 * c + 1, 1]).astype(jnp.bfloat16)
         grad_share(c).start()
 
-        @pl.when(i > 0)
+        @pl.when(i > 1)
         def _():
-            grad_share(i).wait_recv()
-            total = acc[2 * i] + in_sib[i].astype(jnp.float32)
-            out_kv[i] = total.astype(jnp.bfloat16)
-            grad_copy(i).start()
+            pass_on(i - 1)
 
         return carry
 
@@ -265,6 +269,8 @@
 
     out_q[...] = acc_q[1].astype(jnp.bfloat16)
     q_copy.start()
+    if chips > 1:
+        pass_on(chips - 1)
 
     def gather(c, carry):
         grad_copy(c).wait_recv()

time: 21.1 us -> 20.5 us (0.972)
  Pallas kernels: 20.3 us -> 19.7 us
    pallas_call x1, Pallas kernels: 19.6 us -> 19 us  [shards(): pl.pallas_call(functools.partial(kernel, row_size, col_size, heads), out_...]
where the time goes in v4:
time: 20.5 us; the launch traced here: 20.4 us
  Pallas kernels  19.7 us (96%)
  between operations  0.64 us (3%)
    pallas_call x1, Pallas kernels, shards(): pl.pallas_call(functools.partial(kernel, row_size, col_size, heads), out_...  19 us
    pallas_call x1, Pallas kernels, shards(): pl.pallas_call(write_out, out_shape=out_shape, in_specs=[pl.BlockSpec(mem...  0.7 us

profile of v4, /device:TPU:0, one launch (start us, length us, event | category | flops | bytes accessed | tf_op | source)
XLA Modules:
  0.0 20.4 jit_solution(11202364368224418820)
XLA Ops:
  0.6 19.0 %shard_map.112 = (bf16[128,512]{1,0:T(8,128)(2,1)S(1)}, bf16[128,128]{1,0:T(8,128)(2,1)S(1)}, bf16[128,128]{1,0:T(8,128)(2,1)S(1)}) custom-call(bf16[128,512]{1,0:T(8,128)(2,1)} %q_hbm.1, bf16[128,512]{1,0:T(8,128)(2,1)} %d_hbm.1, bf16[128,512]{1,0:T(8,128)(2,1)} %o_hbm.1, bf16[128,128]{1,0:T(8,128)(2,1)} %k_hbm.1, bf16[128,128]{1,0:T(8,128)(2,1)} %v_hbm.1, ...), custom_call_target="tpu_custom_call" | custom-call | flops 1342177280 | bytes 524288 | tf_op jit(solution)/shard_map/pallas_call | solution.py:345
  19.7 0.7 %shard_map.113 = (bf16[128,512]{1,0:T(8,128)(2,1)}, bf16[128,128]{1,0:T(8,128)(2,1)}, bf16[128,128]{1,0:T(8,128)(2,1)}) custom-call(bf16[128,512]{1,0:T(8,128)(2,1)S(1)} %get-tuple-element.6.gq_ref, bf16[128,128]{1,0:T(8,128)(2,1)S(1)} %get-tuple-element.7.gk_ref, bf16[128,128]{1,0:T(8,128)(2,1)S(1)} %get-tuple-element.8.gv_ref), custom_call_target="tpu_custom_call" | custom-call | tf_op jit(solution)/shard_map/pallas_call | solution.py:396
